TPU v7x, 32 devices: a whole 2x2x4 slice. The times are simulated.
32 devices in a mesh: tm: 8 (over z, core), space: 4 (over y, x).
Axes of the slice: x: 2, y: 2, z: 4, core: 2. Of those that a mesh axis runs over, the one named last changes fastest.
Arguments:
- start_states: float32 [8, 2, 12, 192, 256], P('tm', None, None, 'space'), may hold values from -6 to 6
- wet_levels: int32 [192, 256], P('space'), may hold values from 0 to 12
- advection: float32 [192, 256], P('space'), may hold values from 0.05 to 0.3
- forcing: float32 [192, 256], P('space'), may hold values from -6 to 6
- rates: float32 [4, 12], replicated, may hold values from 0.02 to 0.12
Outputs:
- new_states: float32 [8, 2, 12, 192, 256], P('tm', None, None, 'space')
All inputs are finite; a program needn't handle non-finite values.
Results may differ from a plain program's by a relative error of at most 0.00002.
Values sent between devices are 32-bit elements; how exact they have to be, the bound alone decides.
A program may use at most 128 MiB of HBM per device.

v0:
```python
import math

import jax
import jax.numpy as jnp
from jax import lax
from jax.experimental import pallas as pl
from jax.experimental.pallas import tpu as pltpu
from jax.sharding import PartitionSpec as P

STEPS = 4
SECTIONS = 4
COARSEN = 4
RELAX = 0.2
EDGE = 8
LANES = 128
CHUNK = 2
WIDE = COARSEN * SECTIONS
MESH = pl.DeviceIdType.MESH


def season_at(position, year):
    return 1.0 + 0.6 * jnp.sin(2.0 * math.pi * position / year)


def iota(shape, dim):
    return lax.broadcasted_iota(jnp.int32, shape, dim)


def dot(a, b):
    return jnp.dot(a, b, preferred_element_type=jnp.float32)


def split(value):
    parts = []
    for _ in range(3):
        part = value.astype(jnp.bfloat16)
        value = value - part.astype(jnp.float32)
        parts.append(part)
    return parts


def exact(flags, value):
    return jnp.where(flags, value, 0.0).astype(jnp.bfloat16)


def fold_rows(weights, value):
    if weights.shape[1] > value.shape[0]:
        rest = weights.shape[1] - value.shape[0]
        value = jnp.concatenate([value, jnp.zeros((rest, value.shape[1]), value.dtype)], 0)
    return dot(jnp.concatenate([weights] * 3, 1), jnp.concatenate(split(value), 0))


def kernel(
    start_ref, wet_hbm, flow_hbm, forcing_hbm, rates_hbm, out_ref,
    s_ref, state_ref, ring_ref, diag_ref, aux_ref, edge_ref, pack_ref, hr_ref, hl_ref,
    coef_ref, first_ref, jump_ref, x_ref, xl_ref, xr_ref, jl_ref, jr_ref,
    jn_ref, jnl_ref, jnr_ref, coarse_ref, o_ref, ol_ref, or_ref, pl_ref, pr_ref,
    wet_ref, rates_ref, local_sem, send_sem, recv_sem,
):
    _, tracers, levels, nf, lat = out_ref.shape
    nc = nf // COARSEN
    lc = lat // COARSEN
    lanes = 2 * lc
    window = coef_ref.shape[2]
    rows = nf + EDGE
    tm, n_tm = lax.axis_index("tm"), lax.axis_size("tm")
    space, n_space = lax.axis_index("space"), lax.axis_size("space")
    after, before = lax.rem(tm + 1, n_tm), lax.rem(tm + n_tm - 1, n_tm)
    later, earlier = lax.rem(tm + 2, n_tm), lax.rem(tm + n_tm - 2, n_tm)
    right, left = lax.rem(space + 1, n_space), lax.rem(space + n_space - 1, n_space)

    barrier = pltpu.get_barrier_semaphore()
    sources = [(tm, left), (tm, right)]
    sources += [(i, j) for i in (before, earlier) for j in (space, left, right)]
    for i, j in sources:
        pl.semaphore_signal(barrier, inc=1, device_id=(i, j), device_id_type=MESH)

    mid = pl.ds(WIDE, nf)
    loads = [
        pltpu.make_async_copy(src, dst, local_sem.at[i])
        for i, (src, dst) in enumerate((
            (wet_hbm, wet_ref),
            (flow_hbm, aux_ref.at[1, mid, :]),
            (forcing_hbm, aux_ref.at[2, mid, :]),
            (rates_hbm, rates_ref),
            (start_ref.at[0, :, :, pl.ds(0, EDGE), :], edge_ref.at[0]),
            (start_ref.at[0, :, :, pl.ds(nf - EDGE, EDGE), :], edge_ref.at[1]),
        ))
    ]
    for load in loads:
        load.start()
    where = jnp.minimum(iota((8, 128), 1).astype(jnp.float32) + 0.5, STEPS + 0.5)
    where = jnp.where(where > STEPS, STEPS * 0.5, where)
    begin = (before * STEPS).astype(jnp.float32)
    season_ref = season_at(begin + where, STEPS * n_tm)
    begin = (earlier * STEPS).astype(jnp.float32)
    season_before = season_at(begin + where, STEPS * n_tm)
    zero = jnp.zeros((tracers, rows, lat), jnp.float32)
    for step in range(STEPS):
        state_ref[step, :, 0] = zero
        state_ref[step, :, levels + 1] = zero
    for load in loads[:3]:
        load.wait()
    aux_ref[0, mid, :] = wet_ref[...].astype(jnp.float32)
    loads[4].wait()
    loads[5].wait()
    upper_half = iota((EDGE, lat), 0) < COARSEN
    for l in range(levels):
        pack_ref[0, l] = jnp.where(
            upper_half, edge_ref[0, 0, l], pltpu.roll(edge_ref[0, 1, l], COARSEN, 0)
        )
        pack_ref[1, l] = jnp.where(
            upper_half, pltpu.roll(edge_ref[1, 0, l], COARSEN, 0), edge_ref[1, 1, l]
        )
    pl.semaphore_wait(barrier, len(sources))

    def send(index, src, dst, i, j):
        copy = pltpu.make_async_remote_copy(
            src_ref=src, dst_ref=dst, send_sem=send_sem.at[index], recv_sem=recv_sem.at[index],
            device_id=(i, j), device_id_type=MESH,
        )
        copy.start()
        return copy

    sends = [
        send(0, aux_ref.at[:, pl.ds(nf, WIDE), :], aux_ref.at[:, pl.ds(0, WIDE), :], tm, right),
        send(1, aux_ref.at[:, pl.ds(WIDE, WIDE), :],
             aux_ref.at[:, pl.ds(WIDE + nf, WIDE), :], tm, left),
        send(2, pack_ref.at[0], hr_ref, after, left),
        send(3, pack_ref.at[1], hl_ref, after, right),
    ]

    def piece(index):
        part = pl.ds(index * CHUNK, CHUNK)
        return pltpu.make_async_remote_copy(
            src_ref=start_ref.at[0, :, part], dst_ref=s_ref.at[:, part, pl.ds(0, nf), :],
            send_sem=send_sem.at[16 + index], recv_sem=recv_sem.at[16 + index],
            device_id=(after, space), device_id_type=MESH,
        )

    pieces = levels // CHUNK
    for index in range(pieces):
        piece(index).start()

    loads[3].wait()
    sends[0].wait_recv()
    sends[1].wait_recv()
    half = iota((EDGE, lat), 0) < COARSEN
    for i in range(3):
        ring_ref[i, pl.ds(0, nf), :] = aux_ref[i, mid, :]
        ring_ref[i, pl.ds(nf, EDGE), :] = jnp.where(
            half, aux_ref[i, pl.ds(WIDE + nf, EDGE), :], aux_ref[i, pl.ds(WIDE - EDGE, EDGE), :]
        )
    wide = ring_ref[0]
    lane = iota((rows, lat), 1)
    wet_e = pltpu.roll(wide, rows - 1, 0)
    wet_w = pltpu.roll(wide, 1, 0)
    wet_n = jnp.where(lane == lat - 1, 0.0, pltpu.roll(wide, lat - 1, 1))
    wet_s = jnp.where(lane == 0, 0.0, pltpu.roll(wide, 1, 1))
    flow = ring_ref[1]
    for l in range(levels):
        k = rates_ref[0, l]
        west = jnp.where(wet_w > l, 1.0, 0.0)
        count = west
        for other in (wet_e, wet_n, wet_s):
            count = count + jnp.where(other > l, 1.0, 0.0)
        total = 1.0 - k * count - flow * west
        if l:
            total = total - rates_ref[1, l - 1]
        if l < levels - 1:
            total = total - jnp.where(wide > l + 1, rates_ref[1, l], 0.0)
        diag_ref[l] = total
    quarter = 1.0 / COARSEN
    group, folded = iota((lat, lanes), 0) // COARSEN, iota((lat, lanes), 1)
    fold0 = exact(group == folded, quarter)
    fold1 = exact(group + lc == folded, quarter)
    both = fold0 + fold1

    def gather_rows(count, base):
        shape = (window, count)
        return exact(iota(shape, 1) // COARSEN + base == iota(shape, 0), quarter)

    def fold_lat(nutrient, organic):
        pairs = zip(split(nutrient), split(organic))
        return sum(dot(first, fold0) + dot(second, fold1) for first, second in pairs)

    row = iota((window, lanes), 0)
    col = iota((window, lanes), 1)
    inner = (row >= SECTIONS) & (row < SECTIONS + nc)
    to_right = iota((8, lanes), 0) < SECTIONS
    tail = iota((8, lanes), 0) + (window - 8)
    to_left = (tail >= SECTIONS + nc) & (tail < 2 * SECTIONS + nc)

    wide_rows = gather_rows(nf + 2 * WIDE, 0)
    c_flow = fold_rows(wide_rows, fold_lat(aux_ref[1], aux_ref[1])) * (STEPS / COARSEN)
    c_forcing = fold_rows(wide_rows, fold_lat(aux_ref[2], aux_ref[2]))
    wet = aux_ref[0]
    masks = [
        dot(wide_rows, dot(exact(wet > l, 1.0), both).astype(jnp.bfloat16)) for l in range(levels)
    ]
    season = season_ref[0, STEPS]
    is_nutrient = col < lc
    edge_n = (col == lc - 1) | (col == lanes - 1)
    edge_s = (col == 0) | (col == lc)
    for l in range(levels):
        m = masks[l]
        k = rates_ref[0, l] * (STEPS / COARSEN**2)
        g = rates_ref[2, l] * STEPS * season
        g_before = rates_ref[2, l] * STEPS * season_before[0, STEPS]
        r = rates_ref[3, l] * STEPS
        q = RELAX * STEPS if l == 0 else 0.0
        m_w = pltpu.roll(m, 1, 0)
        east = k * pltpu.roll(m, window - 1, 0)
        west = (k + c_flow) * m_w
        north = k * jnp.where(edge_n, 0.0, pltpu.roll(m, lanes - 1, 1))
        south = k * jnp.where(edge_s, 0.0, pltpu.roll(m, 1, 1))
        total = 1.0 - east - west - north - south
        if l < levels - 1:
            down = rates_ref[1, l] * STEPS * masks[l + 1]
            total = total - down
            coef_ref[4, l] = down
        if l:
            up = rates_ref[1, l - 1] * STEPS * masks[l - 1]
            total = total - up
            coef_ref[5, l] = up
        coef_ref[0, l] = east
        coef_ref[1, l] = west
        coef_ref[2, l] = north
        coef_ref[3, l] = south
        coef_ref[6, l] = total
        coef_ref[7, l] = m * jnp.where(is_nutrient, 1.0 - g - q, 1.0 - r)
        coef_ref[8, l] = m * jnp.where(is_nutrient, r, g)
        coef_ref[9, l] = m * jnp.where(is_nutrient, 1.0 - g_before - q, 1.0 - r)
        coef_ref[10, l] = m * jnp.where(is_nutrient, r, g_before)
    surface = masks[0] * jnp.where(is_nutrient, RELAX * STEPS * c_forcing, 0.0)

    sends[2].wait_recv()
    sends[3].wait_recv()
    padded_rows = -(-rows // 16) * 16
    at, ring = iota((window, padded_rows), 0), iota((window, padded_rows), 1)
    start_rows = exact(
        ((ring < nf + COARSEN) & (ring // COARSEN + SECTIONS == at))
        | ((ring >= nf + COARSEN) & (ring < rows) & (at == SECTIONS - 1)),
        quarter,
    )

    centre_rows = gather_rows(nf, SECTIONS)

    def halo_parts(value):
        low = jnp.where(to_right, pltpu.roll(value, window - nc, 0)[:8], 0.0)
        high = jnp.where(to_left, pltpu.roll(value, nc, 0)[window - 8:], 0.0)
        return low, high

    full = -(-(nc + SECTIONS) // 8) * 8

    def put_halos(values, low_ref, high_ref, first=0):
        parts = [halo_parts(value) for value in values]
        for l in range(len(parts) // 2):
            for ref, one, two in zip((low_ref, high_ref), parts[2 * l], parts[2 * l + 1]):
                ref[first + l] = one + pltpu.roll(two, SECTIONS, 0)

    def get_halo(ref, flags, l):
        value = ref[l // 2]
        if l % 2:
            value = pltpu.roll(value, SECTIONS, 0)
        return jnp.where(flags, value, 0.0)

    def widened(value, low_ref, high_ref, l):
        low, high = get_halo(low_ref, to_right, l), get_halo(high_ref, to_left, l)
        pieces = [value[:8] + low, value[8:window - 8]]
        pieces.append(value[window - 8:] + high if full == window else high)
        return jnp.concatenate(pieces, 0)

    def fold_end(first, count):
        part = pl.ds(first, count)
        flat = (count * nf, lat)
        folds = fold_lat(out_ref[0, 0, part].reshape(flat), out_ref[0, 1, part].reshape(flat))
        for j in range(count):
            o_ref[0, first + j] = fold_rows(centre_rows, folds[j * nf:(j + 1) * nf])

    def fold_start(index):
        part = pl.ds(index * CHUNK, CHUNK)
        flat = (CHUNK * rows, lat)
        folds = fold_lat(s_ref[0, part].reshape(flat), s_ref[1, part].reshape(flat))
        for j in range(CHUNK):
            value = fold_rows(start_rows, folds[j * rows:(j + 1) * rows])
            first_ref[index * CHUNK + j] = value

    def arrive(index):
        piece(index).wait_recv()
        for j in range(CHUNK):
            l = index * CHUNK + j
            high, low = hr_ref[l], hl_ref[l]
            s_ref[0, l, pl.ds(nf, EDGE), :] = jnp.where(half, high, pltpu.roll(low, COARSEN, 0))
            s_ref[1, l, pl.ds(nf, EDGE), :] = jnp.where(half, pltpu.roll(high, COARSEN, 0), low)
            here = ring_ref[0] > jnp.asarray(l, jnp.float32)
            for t in range(tracers):
                state_ref[0, t, l + 1] = jnp.where(here, s_ref[t, l], 0.0)

    sub = iota((EDGE, LANES), 0)
    lane = iota((EDGE, LANES), 1)
    blocks = rows // EDGE
    tiles = lat // LANES

    def fine_level(step, l):
        season = season_ref[0, step]
        k, v, g, r = (rates_ref[i, l] for i in range(4))
        upper = rates_ref[1, lax.rem(l + levels - 1, levels)]
        lf = l.astype(jnp.float32)
        grown = g * season
        q = jnp.where(l == 0, RELAX, 0.0)
        kept, stays = 1.0 - grown - q, 1.0 - r
        for x in range(tiles):
            across = pl.ds(x * LANES, LANES)
            cells, norths, souths = [], [], []
            for t in range(tracers):
                cell = [
                    state_ref[step, t, l + 1, pl.ds(b * EDGE, EDGE), across] for b in range(blocks)
                ]
                cells.append(
                    (cell, [pltpu.roll(c, EDGE - 1, 0) for c in cell],
                     [pltpu.roll(c, 1, 0) for c in cell])
                )
            for b in range(blocks if step < STEPS - 1 else blocks - 1):
                down_rows = pl.ds(b * EDGE, EDGE)
                centre = diag_ref[l, down_rows, across]
                speed = ring_ref[1, down_rows, across] + k
                here = ring_ref[0, down_rows, across] > lf
                mixed = []
                for t in range(tracers):
                    cell, fore, back = cells[t]
                    u = cell[b]
                    east = jnp.where(sub == EDGE - 1, fore[(b + 1) % blocks], fore[b])
                    west = jnp.where(sub == 0, back[(b + blocks - 1) % blocks], back[b])
                    if x + 1 < tiles:
                        ahead = state_ref[step, t, l + 1, down_rows, pl.ds((x + 1) * LANES, LANES)]
                        ahead = pltpu.roll(ahead, LANES - 1, 1)
                    else:
                        ahead = 0.0
                    if x:
                        behind = state_ref[step, t, l + 1, down_rows, pl.ds((x - 1) * LANES, LANES)]
                        behind = pltpu.roll(behind, 1, 1)
                    else:
                        behind = 0.0
                    north = jnp.where(lane == LANES - 1, ahead, pltpu.roll(u, LANES - 1, 1))
                    south = jnp.where(lane == 0, behind, pltpu.roll(u, 1, 1))
                    mixed.append(
                        centre * u + k * (east + north + south) + speed * west
                        + v * state_ref[step, t, l + 2, down_rows, across]
                        + upper * state_ref[step, t, l, down_rows, across]
                    )
                nutrient = mixed[0] * kept + r * mixed[1] + q * ring_ref[2, down_rows, across]
                organic = mixed[1] * stays + grown * mixed[0]
                nutrient = jnp.where(here, nutrient, 0.0)
                organic = jnp.where(here, organic, 0.0)
                if step < STEPS - 1:
                    state_ref[step + 1, 0, l + 1, down_rows, across] = nutrient
                    state_ref[step + 1, 1, l + 1, down_rows, across] = organic
                else:
                    out_ref[0, 0, l, down_rows, across] = nutrient
                    out_ref[0, 1, l, down_rows, across] = organic

    lag = 1 - (-STEPS // CHUNK)
    early = (pieces - lag) * CHUNK
    filled = pl.ds(0, full)

    def ends(first, count, index):
        part, pairs = pl.ds(first, count), pl.ds(first // 2, count // 2)
        routes = (
            (o_ref.at[0, part, filled], x_ref.at[0, part, filled], space),
            (ol_ref.at[pairs], xl_ref.at[pairs], right),
            (or_ref.at[pairs], xr_ref.at[pairs], left),
        )
        return [
            pltpu.make_async_remote_copy(
                src_ref=src, dst_ref=dst, send_sem=send_sem.at[index + i],
                recv_sem=recv_sem.at[index + i], device_id=(later, j), device_id_type=MESH,
            )
            for i, (src, dst, j) in enumerate(routes)
        ]

    arrive(0)

    def diagonal(d, carry):
        @pl.when((lax.rem(d + 1, CHUNK) == 0) & (d + 1 < levels))
        def _():
            index = (d + 1) // CHUNK
            fold_start(index - 1)

            @pl.when(index >= lag)
            def _():
                fold_end((index - lag) * CHUNK, CHUNK)

            arrive(index)

            @pl.when(index == pieces - 1)
            def _():
                put_halos([o_ref[0, l] for l in range(early)], ol_ref, or_ref)
                for copy in ends(0, early, 13):
                    copy.start()

        for step in range(STEPS):
            @pl.when((d >= step) & (d < levels + step))
            def _():
                fine_level(step, d - step)

        return carry

    lax.fori_loop(0, levels + STEPS - 1, diagonal, 0)

    fold_end((pieces - lag) * CHUNK, lag * CHUNK)
    put_halos([o_ref[0, l] for l in range(early, levels)], ol_ref, or_ref, early // 2)
    sends += [copy for copy in ends(0, early, 13)]
    for copy in ends(early, levels - early, 4):
        copy.start()
        sends.append(copy)

    def coarse_step(load_level, own=True):
        fields = [load_level(l) for l in range(levels)]
        results = []
        for l in range(levels):
            u = fields[l]
            w = coef_ref[6, l] * u
            w = w + coef_ref[0, l] * pltpu.roll(u, window - 1, 0)
            w = w + coef_ref[1, l] * pltpu.roll(u, 1, 0)
            w = w + coef_ref[2, l] * pltpu.roll(u, lanes - 1, 1)
            w = w + coef_ref[3, l] * pltpu.roll(u, 1, 1)
            if l < levels - 1:
                w = w + coef_ref[4, l] * fields[l + 1]
            if l:
                w = w + coef_ref[5, l] * fields[l - 1]
            kept, mixed = (7, 8) if own else (9, 10)
            value = coef_ref[kept, l] * w + coef_ref[mixed, l] * pltpu.roll(w, lc, 1)
            if l == 0:
                value = value + surface
            results.append(value)
        return results

    fold_start(pieces - 1)
    jumps = []
    for l, value in enumerate(coarse_step(lambda l: first_ref[l])):
        value = jnp.where(inner, value, 0.0)
        first_ref[l] = value
        jump = o_ref[0, l] - value
        jump_ref[l] = jump
        jumps.append(jump)
    put_halos(jumps, pl_ref, pr_ref)
    sends += [
        send(9, jump_ref.at[:, filled], jn_ref.at[:, filled], after, space),
        send(10, pl_ref, jnl_ref, after, right),
        send(11, pr_ref, jnr_ref, after, left),
        send(7, pl_ref, jl_ref, tm, right),
        send(8, pr_ref, jr_ref, tm, left),
    ]

    for copy in sends[4:10]:
        copy.wait_recv()
    results = coarse_step(lambda l: widened(x_ref[0, l], xl_ref, xr_ref, l), own=False)
    for copy in sends[10:13]:
        copy.wait_recv()
    for l in range(levels):
        jump = widened(jn_ref[l], jnl_ref, jnr_ref, l)
        coarse_ref[0, l] = jump
        coarse_ref[1, l] = results[l] + jump
    results = coarse_step(lambda l: coarse_ref[1, l])
    for copy in sends[13:15]:
        copy.wait_recv()
    narrow = full < window
    for l in range(levels):
        value = results[l] + widened(jump_ref[l], jl_ref, jr_ref, l)
        o_ref[1, l] = pltpu.roll(value, window - SECTIONS // 2, 0) if narrow else value
    sends.append(send(12, o_ref.at[1, :, filled], x_ref.at[1, :, filled], later, space))

    def arrived(l):
        value = x_ref[1, l]
        if narrow:
            value = jnp.concatenate([value[:full], jnp.zeros((window - full, lanes), value.dtype)], 0)
            value = pltpu.roll(value, SECTIONS // 2, 0)
        return value

    sends[15].wait_recv()
    results = coarse_step(arrived, own=False)
    for l in range(levels):
        coarse_ref[1, l] = results[l] + coarse_ref[0, l]
    results = coarse_step(lambda l: coarse_ref[1, l])

    chunk = levels // SECTIONS
    shape = (nf, window)
    spread_rows = exact(iota(shape, 0) // COARSEN + SECTIONS == iota(shape, 1), 1.0)
    shape = (lanes, lat)
    group = iota(shape, 1) // COARSEN
    spread0 = exact(group == iota(shape, 0), 1.0)
    spread1 = exact(group + lc == iota(shape, 0), 1.0)
    for c in range(SECTIONS):
        stacked = []
        for l in range(c * chunk, (c + 1) * chunk):
            stacked.append([
                dot(spread_rows, part).astype(jnp.bfloat16) for part in split(results[l] - first_ref[l])
            ])
        parts = [jnp.concatenate(same, 0) for same in zip(*stacked)]
        for t, spread in enumerate((spread0, spread1)):
            value = sum(dot(part, spread) for part in parts).reshape(chunk, nf, lat)
            part = pl.ds(c * chunk, chunk)
            out_ref[0, t, part] = out_ref[0, t, part] + value
    for copy in sends:
        copy.wait_send()
    for index in range(pieces):
        piece(index).wait_send()


def shards(start_states, wet_levels, advection, forcing, rates):
    _, tracers, levels, nf, lat = start_states.shape
    nc = nf // COARSEN
    lanes = 2 * (lat // COARSEN)
    window = -(-(nc + 2 * SECTIONS) // 8) * 8
    rows = nf + EDGE
    f32 = jnp.float32
    packed = pltpu.VMEM((levels, EDGE, lat), f32)
    coarse = pltpu.VMEM((levels, window, lanes), f32)
    edge = pltpu.VMEM((levels // 2, 8, lanes), f32)
    shifts = pltpu.VMEM((2, levels, window, lanes), f32)
    copies = 16 + levels // CHUNK
    vmem = pl.BlockSpec(memory_space=pltpu.VMEM)
    hbm = pl.BlockSpec(memory_space=pltpu.HBM)
    return pl.pallas_call(
        kernel,
        out_shape=jax.ShapeDtypeStruct(start_states.shape, f32),
        in_specs=[hbm] * 5,
        out_specs=vmem,
        scratch_shapes=[
            pltpu.VMEM((tracers, levels, rows, lat), f32),
            pltpu.VMEM((STEPS, tracers, levels + 2, rows, lat), f32),
            pltpu.VMEM((3, rows, lat), f32),
            pltpu.VMEM((levels, rows, lat), f32),
            pltpu.VMEM((3, nf + 2 * WIDE, lat), f32),
            pltpu.VMEM((2, tracers, levels, EDGE, lat), f32),
            pltpu.VMEM((2, levels, EDGE, lat), f32),
            packed, packed,
            pltpu.VMEM((11, levels, window, lanes), f32),
            coarse, coarse, shifts, edge, edge, edge, edge,
            coarse, edge, edge, shifts, shifts, edge, edge, edge, edge,
            pltpu.VMEM((nf, lat), jnp.int32),
            pltpu.SMEM(rates.shape, f32),
            pltpu.SemaphoreType.DMA((6,)),
            pltpu.SemaphoreType.DMA((copies,)),
            pltpu.SemaphoreType.DMA((copies,)),
        ],
        compiler_params=pltpu.CompilerParams(
            collective_id=0, has_side_effects=True, vmem_limit_bytes=64 * 1024 * 1024
        ),
    )(start_states, wet_levels, advection, forcing, rates)

def solution(mesh):
    return jax.shard_map(
        shards,
        mesh=mesh,
        in_specs=(
            P("tm", None, None, "space", None),
            P("space", None),
            P("space", None),
            P("space", None),
            P(),
        ),
        out_specs=P("tm", None, None, "space", None),
        check_vma=False,
    )
```

profile of v0, /device:TPU:0, one launch (start us, length us, event | category | flops | bytes accessed | tf_op | source)
XLA Modules:
  0.0 44.4 jit_solution(17505542758814953157)
XLA Ops:
  0.0 42.0 %shard_map.55 = f32[1,2,12,48,256]{4,3,2,1,0:T(8,128)} custom-call(f32[1,2,12,48,256]{4,3,2,1,0:T(8,128)} %start_ref.1, s32[48,256]{1,0:T(8,128)} %wet_hbm.1, f32[48,256]{1,0:T(8,128)} %flow_hbm.1, f32[48,256]{1,0:T(8,128)} %forcing_hbm.1, f32[4,12]{1,0:T(4,128)} %rates_hbm.1), custom_call_target="tpu_custom_call" | custom-call | tf_op jit(solution)/shard_map/pallas_call | solution.py:525
  42.0 2.4 %copy.7 = f32[1,2,12,48,256]{4,3,2,1,0:T(8,128)} copy(f32[1,2,12,48,256]{4,3,2,1,0:T(8,128)} %shard_map.55) | data formatting | bytes 2359296
where the time goes:
time: 44.6 us; the launch traced here: 44.4 us
  Pallas kernels  42 us (94%)
  local copies, waits for them, and re-layouts  2.37 us (5%)
    pallas_call x1, Pallas kernels, shards(): pl.pallas_call(kernel, out_shape=jax.ShapeDtypeStruct(start_states.shape,...  42 us
    unnamed x1, local copies, waits for them, and re-layouts  2.37 us

commit v1 on v0

--- a/solution.py
+++ b/solution.py
@@ -51,7 +51,7 @@
 
 
 def kernel(
-    start_ref, wet_hbm, flow_hbm, forcing_hbm, rates_hbm, out_ref,
+    start_ref, wet_hbm, flow_hbm, forcing_hbm, rates_hbm, out_hbm, out_ref,
     s_ref, state_ref, ring_ref, diag_ref, aux_ref, edge_ref, pack_ref, hr_ref, hl_ref,
     coef_ref, first_ref, jump_ref, x_ref, xl_ref, xr_ref, jl_ref, jr_ref,
     jn_ref, jnl_ref, jnr_ref, coarse_ref, o_ref, ol_ref, or_ref, pl_ref, pr_ref,
@@ -491,6 +491,7 @@
     group = iota(shape, 1) // COARSEN
     spread0 = exact(group == iota(shape, 0), 1.0)
     spread1 = exact(group + lc == iota(shape, 0), 1.0)
+    stores = []
     for c in range(SECTIONS):
         stacked = []
         for l in range(c * chunk, (c + 1) * chunk):
@@ -502,6 +503,14 @@
             value = sum(dot(part, spread) for part in parts).reshape(chunk, nf, lat)
             part = pl.ds(c * chunk, chunk)
             out_ref[0, t, part] = out_ref[0, t, part] + value
+        part = pl.ds(c * chunk, chunk)
+        store = pltpu.make_async_copy(
+            out_ref.at[:, :, part], out_hbm.at[:, :, part], local_sem.at[6 + c]
+        )
+        store.start()
+        stores.append(store)
+    for store in stores:
+        store.wait()
     for copy in sends:
         copy.wait_send()
     for index in range(pieces):
@@ -520,14 +529,14 @@
     edge = pltpu.VMEM((levels // 2, 8, lanes), f32)
     shifts = pltpu.VMEM((2, levels, window, lanes), f32)
     copies = 16 + levels // CHUNK
-    vmem = pl.BlockSpec(memory_space=pltpu.VMEM)
     hbm = pl.BlockSpec(memory_space=pltpu.HBM)
     return pl.pallas_call(
         kernel,
         out_shape=jax.ShapeDtypeStruct(start_states.shape, f32),
         in_specs=[hbm] * 5,
-        out_specs=vmem,
+        out_specs=hbm,
         scratch_shapes=[
+            pltpu.VMEM((1, tracers, levels, nf, lat), f32),
             pltpu.VMEM((tracers, levels, rows, lat), f32),
             pltpu.VMEM((STEPS, tracers, levels + 2, rows, lat), f32),
             pltpu.VMEM((3, rows, lat), f32),
@@ -541,7 +550,7 @@
             coarse, edge, edge, shifts, shifts, edge, edge, edge, edge,
             pltpu.VMEM((nf, lat), jnp.int32),
             pltpu.SMEM(rates.shape, f32),
-            pltpu.SemaphoreType.DMA((6,)),
+            pltpu.SemaphoreType.DMA((6 + SECTIONS,)),
             pltpu.SemaphoreType.DMA((copies,)),
             pltpu.SemaphoreType.DMA((copies,)),
         ],

time: 44.6 us -> 44.3 us (level)
  no operation moved by 1% of the time
where the time goes in v1:
time: 44.3 us; the launch traced here: 44.1 us
  Pallas kernels  41.7 us (94%)
  local copies, waits for them, and re-layouts  2.37 us (5%)
    pallas_call x1, Pallas kernels, shards(): pl.pallas_call(kernel, out_shape=jax.ShapeDtypeStruct(start_states.shape,...  41.7 us
    unnamed x1, local copies, waits for them, and re-layouts  2.37 us

profile of v1, /device:TPU:0, one launch (start us, length us, event | category | flops | bytes accessed | tf_op | source)
XLA Modules:
  0.0 44.1 jit_solution(8851417228156123230)
XLA Ops:
  0.0 41.7 %shard_map.55 = f32[1,2,12,48,256]{4,3,2,1,0:T(8,128)} custom-call(f32[1,2,12,48,256]{4,3,2,1,0:T(8,128)} %start_ref.1, s32[48,256]{1,0:T(8,128)} %wet_hbm.1, f32[48,256]{1,0:T(8,128)} %flow_hbm.1, f32[48,256]{1,0:T(8,128)} %forcing_hbm.1, f32[4,12]{1,0:T(4,128)} %rates_hbm.1), custom_call_target="tpu_custom_call" | custom-call | tf_op jit(solution)/shard_map/pallas_call | solution.py:533
  41.8 2.4 %copy.7 = f32[1,2,12,48,256]{4,3,2,1,0:T(8,128)} copy(f32[1,2,12,48,256]{4,3,2,1,0:T(8,128)} %shard_map.55) | data formatting | bytes 2359296
